TPU v7x, 1024 devices: a whole 4x8x16 slice. The times are simulated.
1024 devices in a mesh: energy: 64 (over x, y, core), slab: 16 (over z).
Axes of the slice: x: 4, y: 8, z: 16, core: 2. Of those that a mesh axis runs over, the one named last changes fastest.
Arguments:
- green_rows: float32 [2, 128, 4096, 512], P(None, 'energy', 'slab'), may hold values from -6 to 6
- less_surfaces: float32 [2, 128, 4096, 128], P(None, 'energy', 'slab'), may hold values from -6 to 6
- less_diag: float32 [2, 128, 8192], P(None, 'energy', 'slab'), may hold values from -6 to 6
- neighbours: int32 [16, 2, 8, 512], P('slab'), may hold values from 0 to 127
- hopping: float32 [16, 2, 8, 512], P('slab'), may hold values from -0.046875 to 0.046875
- damp: float32 [16, 512], P('slab'), may hold values from 0 to 1
- mode_offset: int32 [8], replicated, may hold values from 1 to 64, as said below
- mode_strength: float32 [8], replicated, may hold values from 0.002 to 0.02
- bose: float32 [8], replicated, may hold values from 0.05 to 2
Outputs:
- correction: float32 [2, 128, 4096, 128], P(None, 'energy', 'slab')
- self_energy: float32 [2, 128, 8192], P(None, 'energy', 'slab')
Inputs may be any that keep to these rules, and one draw needn't show every extreme that they name: `neighbours`: a position within the facing surface of the adjacent slab. `mode_offset`: some mode has offset exactly 64.
All inputs are finite; a program needn't handle non-finite values.
Results may differ from a plain program's by a relative error of at most 0.000071.
Values sent between devices are 32-bit elements; how exact they have to be, the bound alone decides.
A program may use at most 32 MiB of HBM per device.

v0:
```python
import jax
import jax.numpy as jnp
from jax import lax
from jax.sharding import PartitionSpec as P

PRECISE = lax.Precision.HIGHEST


def with_halo(block, sides, width):
    for axis, dim in sides:
        count = lax.axis_size(axis)
        forward = [(i, i + 1) for i in range(count - 1)]
        backward = [(target, source) for source, target in forward]
        low = lax.ppermute(
            lax.slice_in_dim(block, block.shape[dim] - width, None, axis=dim), axis, forward
        )
        high = lax.ppermute(lax.slice_in_dim(block, 0, width, axis=dim), axis, backward)
        block = jnp.concatenate([low, block, high], axis=dim)
    return block


def sent_to_all(array, axis):
    size = lax.axis_size(axis)
    return lax.all_to_all(
        jnp.broadcast_to(array[None], (size, *array.shape)), axis, 0, 0, tiled=True
    )


def gathered_once(array, axis):
    leaves = jax.tree.leaves(array)
    order = sorted(range(len(leaves)), key=lambda k: -leaves[k].size)
    width = (1, *leaves[order[0]].shape)[-1]
    lines = [
        jnp.pad(leaves[k].reshape(-1), (0, -leaves[k].size % width)).reshape(-1, width)
        for k in order
    ]
    both, at, found = (sent_to_all(jnp.concatenate(lines), axis), 0, {})
    for k, line in zip(order, lines):
        slab = both[:, at : at + len(line)].reshape(len(both), -1)
        found[k] = slab[:, : leaves[k].size].reshape(-1, *leaves[k].shape)
        at += len(line)
    numbers = iter(range(len(leaves)))
    return jax.tree.map(lambda _: found[next(numbers)], array)


def combined_pairwise(pieces, combine):
    while len(jax.tree.leaves(pieces)[0]) > 1:
        pieces = jax.vmap(combine)(
            *(jax.tree.map(lambda part: part[side::2], pieces) for side in (0, 1))
        )
    return jax.tree.map(lambda part: part[0], pieces)


def prefix_2(array, axis, combine, identity):
    size, mine = (lax.axis_size(axis), lax.axis_index(axis))
    passed = jnp.arange(size) < mine

    def kept(part, zero, own):
        part = jnp.where(
            passed.reshape(-1, *(1 for _ in own.shape)), part, jnp.asarray(zero, own.dtype)
        )
        return part

    pieces = gathered_once(array, axis)
    return combined_pairwise(jax.tree.map(kept, pieces, identity, array), combine)


def in_order(blocks, dim):
    dims = list(blocks.shape[1:])
    dims[dim] *= blocks.shape[0]
    return jnp.moveaxis(blocks, 0, dim).reshape(dims)


def collect(array, axis, dim):
    blocks = sent_to_all(array, axis)
    return in_order(blocks, dim)


def coupling_single(neighbour_ids, weights, surface):
    slot_ids = lax.broadcasted_iota(jnp.int32, (1, 1, surface, 1), 2)
    one_hot = (neighbour_ids[:, :, None, :] == slot_ids).astype(jnp.float32)
    return jnp.sum(one_hot * weights[:, :, None, :], axis=1)


def phonon_kernel(mode_offset, mode_strength, bose, energy_count):
    row_ids = lax.broadcasted_iota(jnp.int32, (1, energy_count, energy_count), 1)
    column_ids = lax.broadcasted_iota(jnp.int32, (1, energy_count, energy_count), 2)
    shifts = mode_offset[:, None, None]
    emitted = (column_ids == row_ids + shifts).astype(jnp.float32)
    absorbed = (column_ids == row_ids - shifts).astype(jnp.float32)
    occupied = bose[:, None, None]
    return jnp.sum(
        mode_strength[:, None, None] * ((occupied + 1.0) * emitted + occupied * absorbed), axis=0
    )


def complex_product(left_factor, right_factor, pattern):
    real_part = jnp.einsum(
        pattern, left_factor[0], right_factor[0], precision=PRECISE
    ) - jnp.einsum(pattern, left_factor[1], right_factor[1], precision=PRECISE)
    imag_part = jnp.einsum(
        pattern, left_factor[0], right_factor[1], precision=PRECISE
    ) + jnp.einsum(pattern, left_factor[1], right_factor[0], precision=PRECISE)
    return jnp.stack([real_part, imag_part])


def block_outer(left_factor, right_factor, surface):
    shape_in = left_factor.shape
    block_count = shape_in[2] // surface
    left_blocks = left_factor.reshape(shape_in[0], shape_in[1], block_count, surface, shape_in[3])
    right_blocks = right_factor.reshape(
        shape_in[0], shape_in[1], block_count, surface, right_factor.shape[3]
    )
    pattern = "abik,abjk->abij"
    real_part = jnp.einsum(
        pattern, left_blocks[0], right_blocks[0], precision=PRECISE
    ) + jnp.einsum(pattern, left_blocks[1], right_blocks[1], precision=PRECISE)
    imag_part = jnp.einsum(
        pattern, left_blocks[1], right_blocks[0], precision=PRECISE
    ) - jnp.einsum(pattern, left_blocks[0], right_blocks[1], precision=PRECISE)
    return jnp.stack([real_part, imag_part]).reshape(shape_in[0], shape_in[1], shape_in[2], surface)


def local(
    green_rows,
    less_surfaces,
    less_diag,
    neighbours,
    hopping,
    damp,
    mode_offset,
    mode_strength,
    bose,
):
    energy_count = green_rows.shape[1]
    surface = less_surfaces.shape[3]
    total_energies = energy_count * lax.axis_size("energy")
    padded = with_halo(less_surfaces, (("slab", 2),), surface)
    couple = coupling_single(neighbours[0], hopping[0], surface)
    coupled_lower = jnp.einsum("cerj,qj->cerq", green_rows, couple[0], precision=PRECISE)
    coupled_upper = jnp.einsum("cerj,qj->cerq", green_rows, couple[1], precision=PRECISE)

    def compose(earlier_map, later_map):
        return (earlier_map[0] * later_map[0], later_map[0] * earlier_map[1] + later_map[1])

    identity = (jnp.ones_like(damp[0]), jnp.zeros_like(less_diag))
    prefix = prefix_2((damp[0], less_diag), "slab", compose, identity)
    carried = prefix[1]
    occupation = less_diag + carried
    kernel = phonon_kernel(mode_offset, mode_strength, bose, total_energies)
    own_rows = lax.dynamic_slice_in_dim(
        kernel, lax.axis_index("energy") * energy_count, energy_count, 0
    )
    phonon_sigma = jnp.zeros_like(occupation) + jnp.einsum(
        "ef,cfo->ceo", own_rows, collect(occupation, "energy", 1), precision=PRECISE
    )
    scaled = jnp.stack(
        [
            green_rows[0] * phonon_sigma[0][:, None, :]
            - green_rows[1] * phonon_sigma[1][:, None, :],
            green_rows[0] * phonon_sigma[1][:, None, :]
            + green_rows[1] * phonon_sigma[0][:, None, :],
        ]
    )
    lower_block = padded[:, :, :surface]
    upper_block = padded[:, :, padded.shape[2] - surface :]
    weighted_lower = complex_product(coupled_lower, lower_block, "erq,eqt->ert")
    weighted_upper = complex_product(coupled_upper, upper_block, "erq,eqt->ert")
    correction = block_outer(scaled, green_rows, surface)
    correction = correction + block_outer(weighted_lower, coupled_lower, surface)
    correction = correction + block_outer(weighted_upper, coupled_upper, surface)
    return (correction, phonon_sigma)


def solution(mesh):
    placed = (
        P(None, "energy", "slab", None),
        P(None, "energy", "slab", None),
        P(None, "energy", "slab"),
        P("slab", None, None, None),
        P("slab", None, None, None),
        P("slab", None),
        P(),
        P(),
        P(),
    )
    return jax.shard_map(
        local,
        mesh=mesh,
        in_specs=placed,
        out_specs=(P(None, "energy", "slab", None), P(None, "energy", "slab")),
        check_vma=False,
    )
```

profile of v0, /device:TPU:1, one launch (start us, length us, event | category | flops | bytes accessed | tf_op | source)
XLA Modules:
  0.0 103.8 jit_solution(5068041820446769982)
XLA Ops:
  2.9 19.5 %all-to-all-start = ((f32[16,5,512]{2,1,0:T(8,128)}), f32[16,5,512]{2,1,0:T(8,128)}, u32[]{:S(2)}, u32[]{:S(2)}) async-start(f32[16,5,512]{2,1,0:T(8,128)} %broadcast_in_dim.29), calls=%async_computation | async-start | bytes 524288 | tf_op jit(solution)/shard_map/all_to_all | solution.py:24
  22.4 1.9 %fusion.38 = (f32[2,2,128,128]{3,2,1,0:T(8,128)}, f32[2,2,128,128]{3,2,1,0:T(8,128)}) fusion(f32[2,2,256,128]{3,2,1,0:T(8,128)} %param.10), kind=kLoop, calls=%fused_computation.78 | loop fusion | bytes 1048576 | tf_op jit(solution)/shard_map/slice | solution.py:17
  24.3 1.3 %collective-permute-start.1 = (f32[2,2,128,128]{3,2,1,0:T(8,128)}, f32[2,2,128,128]{3,2,1,0:T(8,128)}, u32[]{:S(2)}, u32[]{:S(2)}) collective-permute-start(f32[2,2,128,128]{3,2,1,0:T(8,128)} %get-tuple-element.6), channel_id=1, source_target_pairs={{1,0},{2,1},{3,2},{4,3},{5,4},{6,5},{7,6},{8,7},{9,8},{10,9},{11,1... | collective-permute-start | bytes 786440 | tf_op jit(solution)/shard_map/ppermute | solution.py:17
  25.5 4.7 %collective-permute-start = (f32[2,2,128,128]{3,2,1,0:T(8,128)}, f32[2,2,128,128]{3,2,1,0:T(8,128)}, u32[]{:S(2)}, u32[]{:S(2)}) collective-permute-start(f32[2,2,128,128]{3,2,1,0:T(8,128)} %get-tuple-element.7), channel_id=1, source_target_pairs={{0,1},{1,2},{2,3},{3,4},{4,5},{5,6},{6,7},{7,8},{8,9},{9,10},{10,1... | collective-permute-start | bytes 786440 | tf_op jit(solution)/shard_map/ppermute | solution.py:14
  30.2 1.4 %select_reduce_fusion = f32[2,128,512]{2,1,0:T(8,128)S(1)} fusion(f32[2,8,512]{2,1,0:T(8,128)} %bitcast.142, s32[2,8,512]{2,1,0:T(8,128)} %bitcast.143), kind=kLoop, calls=%fused_computation | loop fusion | flops 3014656 | bytes 589824 | tf_op jit(solution)/shard_map/reduce_sum | solution.py:82
  31.6 2.3 %convolution_bitcast_fusion = f32[2,2,256,128]{2,3,1,0:T(8,128)S(1)} fusion(f32[2,2,256,512]{3,2,1,0:T(8,128)S(1)} %copy-done, f32[2,128,512]{2,1,0:T(8,128)S(1)} %select_reduce_fusion), kind=kOutput, calls=%fused_computation.2 | convolution fusion | flops 805306368 | bytes 2883584 | tf_op jit(solution)/shard_map/cerj,qj->cerq/dot_general | solution.py:141
  33.9 2.3 %convolution_bitcast_fusion.1 = f32[2,2,256,128]{2,3,1,0:T(8,128)S(1)} fusion(f32[2,2,256,512]{3,2,1,0:T(8,128)S(1)} %copy-done, f32[2,128,512]{2,1,0:T(8,128)S(1)} %select_reduce_fusion), kind=kOutput, calls=%fused_computation.3 | convolution fusion | flops 805306368 | bytes 2883584 | tf_op jit(solution)/shard_map/cerj,qj->cerq/dot_general | solution.py:140
  39.9 1.7 %fusion.36 = (f32[1,2,256,512]{3,2,1,0:T(8,128)S(1)}, f32[1,2,256,512]{3,2,1,0:T(8,128)S(1)}) fusion(f32[2,2,256,512]{3,2,1,0:T(8,128)} %param.9), kind=kLoop, calls=%fused_computation.76 | loop fusion | bytes 4194304 | tf_op jit(solution)/shard_map/slice | solution.py:160
  41.6 1.5 %fusion.13 = f32[2,256,128]{2,1,0:T(8,128)S(1)} fusion(f32[2,2,128,128]{3,2,1,0:T(8,128)} %collective-permute-done.1, f32[2,2,256,128]{2,3,1,0:T(8,128)S(1)} %convolution_bitcast_fusion), kind=kOutput, calls=%fused_computation.36 | convolution fusion | flops 100663296 | bytes 655360 | tf_op jit(solution)/shard_map/erq,eqt->ert/dot_general | solution.py:100
  43.2 1.5 %fusion.11 = f32[2,256,128]{2,1,0:T(8,128)S(1)} fusion(f32[2,2,128,128]{3,2,1,0:T(8,128)} %collective-permute-done.1, f32[2,2,256,128]{2,3,1,0:T(8,128)S(1)} %convolution_bitcast_fusion), kind=kOutput, calls=%fused_computation.34 | convolution fusion | flops 100663296 | bytes 655360 | tf_op jit(solution)/shard_map/erq,eqt->ert/dot_general | solution.py:103
  44.7 1.5 %convolution_subtract_fusion.1 = f32[2,256,128]{2,1,0:T(8,128)S(1)} fusion(f32[2,256,128]{2,1,0:T(8,128)S(1)} %fusion.13, f32[2,2,128,128]{3,2,1,0:T(8,128)} %collective-permute-done.1, f32[2,2,256,128]{2,3,1,0:T(8,128)S(1)} %convolution_bitcast_fusion), kind=kOutput, calls=%fused_computation.7 | convolution fusion | flops 100728832 | bytes 917504 | tf_op jit(solution)/shard_map/erq,eqt->ert/dot_general | solution.py:98
  46.2 1.6 %convolution_add_fusion.1 = f32[2,256,128]{2,1,0:T(8,128)S(1)} fusion(f32[2,256,128]{2,1,0:T(8,128)S(1)} %fusion.11, f32[2,2,128,128]{3,2,1,0:T(8,128)} %collective-permute-done.1, f32[2,2,256,128]{2,3,1,0:T(8,128)S(1)} %convolution_bitcast_fusion), kind=kOutput, calls=%fused_computation.6 | convolution fusion | flops 100728832 | bytes 917504 | tf_op jit(solution)/shard_map/erq,eqt->ert/dot_general | solution.py:101
  47.8 1.4 %fusion.42 = f32[2,2,128,128]{3,2,1,0:T(8,128)} fusion(f32[2,2,128,128]{3,2,1,0:T(8,128)S(1)} %bitcast.124, f32[2,2,128,128]{3,2,1,0:T(8,128)S(1)} %bitcast.122), kind=kOutput, calls=%fused_computation.82 | convolution fusion | flops 100663296 | bytes 786432 | tf_op jit(solution)/shard_map/abik,abjk->abij/dot_general | solution.py:115
  49.2 1.4 %fusion.43 = f32[2,2,128,128]{3,2,1,0:T(8,128)} fusion(f32[2,2,128,128]{3,2,1,0:T(8,128)S(1)} %bitcast.126, f32[2,2,128,128]{3,2,1,0:T(8,128)S(1)} %bitcast.123), kind=kOutput, calls=%fused_computation.83 | convolution fusion | flops 100663296 | bytes 786432 | tf_op jit(solution)/shard_map/abik,abjk->abij/dot_general | solution.py:118
  50.5 1.5 %fusion.19 = f32[2,256,128]{2,1,0:T(8,128)S(1)} fusion(f32[2,2,128,128]{3,2,1,0:T(8,128)} %collective-permute-done, f32[2,2,256,128]{2,3,1,0:T(8,128)S(1)} %convolution_bitcast_fusion.1), kind=kOutput, calls=%fused_computation.42 | convolution fusion | flops 100663296 | bytes 655360 | tf_op jit(solution)/shard_map/erq,eqt->ert/dot_general | solution.py:100
  52.0 1.5 %convolution_subtract_fusion.3 = f32[2,256,128]{2,1,0:T(8,128)S(1)} fusion(f32[2,256,128]{2,1,0:T(8,128)S(1)} %fusion.19, f32[2,2,128,128]{3,2,1,0:T(8,128)} %collective-permute-done, f32[2,2,256,128]{2,3,1,0:T(8,128)S(1)} %convolution_bitcast_fusion.1), kind=kOutput, calls=%fused_computation.11 | convolution fusion | flops 100728832 | bytes 917504 | tf_op jit(solution)/shard_map/erq,eqt->ert/dot_general | solution.py:98
  53.5 1.5 %fusion.17 = f32[2,256,128]{2,1,0:T(8,128)S(1)} fusion(f32[2,2,128,128]{3,2,1,0:T(8,128)} %collective-permute-done, f32[2,2,256,128]{2,3,1,0:T(8,128)S(1)} %convolution_bitcast_fusion.1), kind=kOutput, calls=%fused_computation.40 | convolution fusion | flops 100663296 | bytes 655360 | tf_op jit(solution)/shard_map/erq,eqt->ert/dot_general | solution.py:103
  55.0 1.4 %fusion.40 = f32[2,2,128,128]{3,2,1,0:T(8,128)} fusion(f32[2,2,128,128]{3,2,1,0:T(8,128)S(1)} %bitcast.128, f32[2,2,128,128]{3,2,1,0:T(8,128)S(1)} %bitcast.120), kind=kOutput, calls=%fused_computation.80 | convolution fusion | flops 100663296 | bytes 786432 | tf_op jit(solution)/shard_map/abik,abjk->abij/dot_general | solution.py:115
  56.4 1.5 %convolution_add_fusion.3 = f32[2,256,128]{2,1,0:T(8,128)S(1)} fusion(f32[2,256,128]{2,1,0:T(8,128)S(1)} %fusion.17, f32[2,2,128,128]{3,2,1,0:T(8,128)} %collective-permute-done, f32[2,2,256,128]{2,3,1,0:T(8,128)S(1)} %convolution_bitcast_fusion.1), kind=kOutput, calls=%fused_computation.10 | convolution fusion | flops 100728832 | bytes 917504 | tf_op jit(solution)/shard_map/erq,eqt->ert/dot_general | solution.py:101
  66.1 12.0 %all-to-all-start.1 = ((f32[64,2,2,512]{3,2,1,0:T(2,128)}), f32[64,2,2,512]{3,2,1,0:T(2,128)}, u32[]{:S(2)}, u32[]{:S(2)}) async-start(f32[64,2,2,512]{3,2,1,0:T(2,128)} %broadcast_in_dim.50), calls=%async_computation.1 | async-start | bytes 1048576 | tf_op jit(solution)/shard_map/all_to_all | solution.py:24
  78.8 2.4 %convolution_add_fusion = f32[2,2,128,128]{3,2,1,0:T(8,128)} fusion(f32[2,2,128,128]{3,2,1,0:T(8,128)} %fusion.42, f32[2,2,128,128]{3,2,1,0:T(8,128)S(1)} %bitcast.127, f32[2,2,128,128]{3,2,1,0:T(8,128)} %bitcast.132), kind=kOutput, calls=%fused_computation.5 | convolution fusion | flops 100728832 | bytes 1048576 | tf_op jit(solution)/shard_map/abik,abjk->abij/dot_general | solution.py:117
  81.2 2.4 %convolution_subtract_fusion = f32[2,2,128,128]{3,2,1,0:T(8,128)} fusion(f32[2,2,128,128]{3,2,1,0:T(8,128)} %fusion.43, f32[2,2,128,128]{3,2,1,0:T(8,128)S(1)} %bitcast.125, f32[2,2,128,128]{3,2,1,0:T(8,128)} %bitcast.133), kind=kOutput, calls=%fused_computation.4 | convolution fusion | flops 100728832 | bytes 1048576 | tf_op jit(solution)/shard_map/abik,abjk->abij/dot_general | solution.py:120
  83.6 1.4 %convolution_add_fusion.2 = f32[2,2,128,128]{3,2,1,0:T(8,128)} fusion(f32[2,2,128,128]{3,2,1,0:T(8,128)S(1)} %copy-done.7, f32[2,2,128,128]{3,2,1,0:T(8,128)S(1)} %bitcast.131, f32[2,2,128,128]{3,2,1,0:T(8,128)S(1)} %bitcast.134), kind=kOutput, calls=%fused_computation.9 | convolution fusion | flops 100728832 | bytes 1048576 | tf_op jit(solution)/shard_map/abik,abjk->abij/dot_general | solution.py:117
  85.7 9.7 %all-to-all-done.1 = f32[64,2,2,512]{3,2,1,0:T(2,128)} async-done(((f32[64,2,2,512]{3,2,1,0:T(2,128)}), f32[64,2,2,512]{3,2,1,0:T(2,128)}, u32[]{:S(2)}, u32[]{:S(2)}) %all-to-all-start.1) | async-done | bytes 524320 | tf_op jit(solution)/shard_map/all_to_all | solution.py:24
  (79 shorter events, 23.7 us)
Async XLA Ops:
  0.6 31.0 %copy-start = (f32[2,2,256,512]{3,2,1,0:T(8,128)S(1)}, f32[2,2,256,512]{3,2,1,0:T(8,128)}, u32[]{:S(2)}) copy-start(f32[2,2,256,512]{3,2,1,0:T(8,128)} %param.9) | copy-start | bytes 6291460
  2.9 55.0 %all-to-all-start = ((f32[16,5,512]{2,1,0:T(8,128)}), f32[16,5,512]{2,1,0:T(8,128)}, u32[]{:S(2)}, u32[]{:S(2)}) async-start(f32[16,5,512]{2,1,0:T(8,128)} %broadcast_in_dim.29), calls=%async_computation | async-start | bytes 524288 | tf_op jit(solution)/shard_map/all_to_all | solution.py:24
  24.3 17.4 %collective-permute-start.1 = (f32[2,2,128,128]{3,2,1,0:T(8,128)}, f32[2,2,128,128]{3,2,1,0:T(8,128)}, u32[]{:S(2)}, u32[]{:S(2)}) collective-permute-start(f32[2,2,128,128]{3,2,1,0:T(8,128)} %get-tuple-element.6), channel_id=1, source_target_pairs={{1,0},{2,1},{3,2},{4,3},{5,4},{6,5},{7,6},{8,7},{9,8},{10,9},{11,1... | collective-permute-start | bytes 786440 | tf_op jit(solution)/shard_map/ppermute | solution.py:17
  25.5 25.0 %collective-permute-start = (f32[2,2,128,128]{3,2,1,0:T(8,128)}, f32[2,2,128,128]{3,2,1,0:T(8,128)}, u32[]{:S(2)}, u32[]{:S(2)}) collective-permute-start(f32[2,2,128,128]{3,2,1,0:T(8,128)} %get-tuple-element.7), channel_id=1, source_target_pairs={{0,1},{1,2},{2,3},{3,4},{4,5},{5,6},{6,7},{7,8},{8,9},{9,10},{10,1... | collective-permute-start | bytes 786440 | tf_op jit(solution)/shard_map/ppermute | solution.py:14
  33.9 2.3 %copy-start.14 = (f32[8]{0:T(128)S(1)}, f32[8]{0:T(128)}, u32[]{:S(2)}) copy-start(f32[8]{0:T(128)} %param.17) | copy-start | bytes 100
  36.2 22.7 %copy-start.13 = (pred[16]{0:T(512)(128)(4,1)}, pred[16]{0:T(512)(128)(4,1)S(1)}, u32[]{:S(2)}) copy-start(pred[16]{0:T(512)(128)(4,1)S(1)} %iota_compare_fusion.1) | copy-start | bytes 52
  36.3 2.8 %copy-start.15 = (s32[8]{0:T(128)S(1)}, s32[8]{0:T(128)}, u32[]{:S(2)}) copy-start(s32[8]{0:T(128)} %param.15) | copy-start | bytes 100
  36.3 2.7 %copy-start.16 = (f32[8]{0:T(128)S(1)}, f32[8]{0:T(128)}, u32[]{:S(2)}) copy-start(f32[8]{0:T(128)} %param.16) | copy-start | bytes 100
  41.6 6.2 %copy-start.1 = (f32[1,2,256,128]{3,2,1,0:T(8,128)S(1)}, f32[1,2,256,128]{3,2,1,0:T(8,128)}, u32[]{:S(2)}) copy-start(f32[1,2,256,128]{3,2,1,0:T(8,128)} %copy.74) | copy-start | bytes 786436
  46.2 8.9 %copy-start.2 = (f32[2,256,128]{2,1,0:T(8,128)}, f32[2,256,128]{2,1,0:T(8,128)S(1)}, u32[]{:S(2)}) copy-start(f32[2,256,128]{2,1,0:T(8,128)S(1)} %convolution_subtract_fusion.1) | copy-start | bytes 786436
  47.8 8.6 %copy-start.4 = (f32[2,256,128]{2,1,0:T(8,128)}, f32[2,256,128]{2,1,0:T(8,128)S(1)}, u32[]{:S(2)}) copy-start(f32[2,256,128]{2,1,0:T(8,128)S(1)} %convolution_add_fusion.1) | copy-start | bytes 786436
  57.9 20.9 %copy-start.5 = (f32[2,256,128]{2,1,0:T(8,128)S(1)}, f32[2,256,128]{2,1,0:T(8,128)}, u32[]{:S(2)}) copy-start(f32[2,256,128]{2,1,0:T(8,128)} %copy-done.4) | copy-start | bytes 786436
  59.1 1.3 %copy-start.11 = (f32[4,512]{1,0:T(4,128)}, f32[4,512]{1,0:T(4,128)S(1)}, u32[]{:S(2)}) copy-start(f32[4,512]{1,0:T(4,128)S(1)} %slice.155) | copy-start | bytes 24580
  61.5 19.8 %copy-start.3 = (f32[2,256,128]{2,1,0:T(8,128)S(1)}, f32[2,256,128]{2,1,0:T(8,128)}, u32[]{:S(2)}) copy-start(f32[2,256,128]{2,1,0:T(8,128)} %copy-done.2) | copy-start | bytes 786436
  66.1 29.2 %all-to-all-start.1 = ((f32[64,2,2,512]{3,2,1,0:T(2,128)}), f32[64,2,2,512]{3,2,1,0:T(2,128)}, u32[]{:S(2)}, u32[]{:S(2)}) async-start(f32[64,2,2,512]{3,2,1,0:T(2,128)} %broadcast_in_dim.50), calls=%async_computation.1 | async-start | bytes 1048576 | tf_op jit(solution)/shard_map/all_to_all | solution.py:24
  78.1 5.5 %copy-start.6 = (f32[1,2,256,128]{3,2,1,0:T(8,128)S(1)}, f32[1,2,256,128]{3,2,1,0:T(8,128)}, u32[]{:S(2)}) copy-start(f32[1,2,256,128]{3,2,1,0:T(8,128)} %copy.73) | copy-start | bytes 786436
  78.1 5.5 %copy-start.7 = (f32[2,2,128,128]{3,2,1,0:T(8,128)S(1)}, f32[2,2,128,128]{3,2,1,0:T(8,128)}, u32[]{:S(2)}) copy-start(f32[2,2,128,128]{3,2,1,0:T(8,128)} %fusion.40) | copy-start | bytes 786436
  97.9 2.4 %copy-start.12 = (f32[2,2,512]{2,1,0:T(2,128)}, f32[2,2,512]{2,1,0:T(2,128)S(1)}, u32[]{:S(2)}) copy-start(f32[2,2,512]{2,1,0:T(2,128)S(1)} %convolution_bitcast_fusion.2) | copy-start | bytes 24580
  101.6 1.3 %copy-start.8 = (f32[2,2,128,128]{3,2,1,0:T(8,128)S(1)}, f32[2,2,128,128]{3,2,1,0:T(8,128)}, u32[]{:S(2)}) copy-start(f32[2,2,128,128]{3,2,1,0:T(8,128)} %convolution_add_fusion) | copy-start | bytes 786436
  101.6 1.3 %copy-start.9 = (f32[2,2,128,128]{3,2,1,0:T(8,128)S(1)}, f32[2,2,128,128]{3,2,1,0:T(8,128)}, u32[]{:S(2)}) copy-start(f32[2,2,128,128]{3,2,1,0:T(8,128)} %convolution_subtract_fusion) | copy-start | bytes 786436
  101.6 1.3 %copy-start.10 = (f32[2,2,128,128]{3,2,1,0:T(8,128)S(1)}, f32[2,2,128,128]{3,2,1,0:T(8,128)}, u32[]{:S(2)}) copy-start(f32[2,2,128,128]{3,2,1,0:T(8,128)} %convolution_add_fusion.2) | copy-start | bytes 786436
where the time goes:
time: 105 us; the launch traced here: 104 us
  starting transfers between devices  37.4 us (36%)
  matrix products  34.2 us (33%)
  local copies, waits for them, and re-layouts  13.7 us (13%)
  waiting for transfers between devices  9.7 us (9%)
  other arithmetic  7.63 us (7%)
  between operations  1.1 us (1%)
    all_to_all x2, starting transfers between devices, sent_to_all(): lax.all_to_all(jnp.broadcast_to(array[None], (size, *array.shape)), axis,...  31.5 us
    all_to_all x2, waiting for transfers between devices, sent_to_all(): lax.all_to_all(jnp.broadcast_to(array[None], (size, *array.shape)), axis,...  9.7 us
    dot_general x3, matrix products, block_outer(): jnp.einsum(pattern, left_blocks[1], right_blocks[1], precision=PRECISE)  4.99 us
    ppermute x1, starting transfers between devices, with_halo(): lax.ppermute(lax.slice_in_dim(block, block.shape[dim] - width, None, axis...  4.69 us
    dot_general x3, matrix products, block_outer(): jnp.einsum(pattern, left_blocks[0], right_blocks[1], precision=PRECISE)  4.27 us
    dot_general x3, matrix products, block_outer(): jnp.einsum(pattern, left_blocks[0], right_blocks[0], precision=PRECISE)  3.95 us
    dot_general x3, matrix products, block_outer(): jnp.einsum(pattern, left_blocks[1], right_blocks[0], precision=PRECISE)  3.24 us
    dot_general x2, matrix products, complex_product(): jnp.einsum(pattern, left_factor[0], right_factor[1], precision=PRECISE)  3.08 us
  transfers between devices with their start and end apart: 4, of which 1 were waited for; matrix products, arithmetic and copies ran while one was open for 35% of the time, Pallas kernels for 0%

commit v1 on v0

v1 whole, which is shorter than its diff:
```python
import jax
import jax.numpy as jnp
from jax import lax
from jax.experimental import pallas as pl
from jax.experimental.pallas import tpu as pltpu
from jax.sharding import PartitionSpec as P

MESH = pl.DeviceIdType.MESH
F32 = jnp.float32
BF16 = jnp.bfloat16
NX, NY, NC, NZ = 4, 8, 2, 16
GROUP = 4
ORB = 512
SURF = 128
NB = 8
MODES = 8


def split(value):
    high = value.astype(BF16)
    return high, (value - high.astype(F32)).astype(BF16)


def dot3(left_high, left_low, right_high, right_low, transposed):
    dims = (((1,), (1 if transposed else 0,)), ((), ()))

    def one(left, right):
        return lax.dot_general(left, right, dims, preferred_element_type=F32)

    return one(left_high, right_low) + one(left_low, right_high) + one(left_high, right_high)


def kernel(
    green_hbm, less_hbm, diag_hbm, near_hbm, hop_hbm, damp_hbm, offset_hbm, strength_hbm, bose_hbm,
    out_ref, sigma_ref,
    green, gh, gl, ch, cl, cph, cpl, wh, wl,
    near, hop, damp, diag, offset, strength, bose,
    gathered, stacked, partial, reduced, zout, zgroup, ztotal, low_block, up_block,
    local_sem, xc_sem, y_sem, zs_sem, zr_sem, lead_sem, total_sem, halo_send, halo_recv,
):
    e, s = lax.axis_index("energy"), lax.axis_index("slab")
    x, y, c = e // (NY * NC), lax.rem(e // NC, NY), lax.rem(e, NC)
    lane, group = lax.rem(s, GROUP), s // GROUP

    def at(px, py, pc):
        return (px * NY + py) * NC + pc

    xc_peers = []
    for d in range(1, NX * NC):
        px, pc = lax.rem(x + d // NC, NX), lax.rem(c + d % NC, NC)
        xc_peers.append((at(px, y, pc), s))
    y_peers = [(lax.rem(y + d, NY), (at(x, lax.rem(y + d, NY), c), s)) for d in range(1, NY)]

    barrier = pltpu.get_barrier_semaphore()

    def tell(device):
        pl.semaphore_signal(barrier, inc=1, device_id=device, device_id_type=MESH)

    for _, device in y_peers:
        tell(device)
    for device in xc_peers:
        tell(device)

    @pl.when(s < NZ - 1)
    def _():
        tell((e, s + 1))

    for k in range(GROUP - 1):

        @pl.when(k < lane)
        def _(k=k):
            tell((e, group * GROUP + k))

    for k in range(NZ // GROUP - 1):

        @pl.when(k < group)
        def _(k=k):
            tell((e, jnp.int32(k * GROUP + GROUP - 1)))

    pairs = [
        (diag_hbm, diag), (damp_hbm, damp), (offset_hbm, offset), (strength_hbm, strength), (bose_hbm, bose),
        (near_hbm, near), (hop_hbm, hop), (green_hbm, green),
    ]
    loads = [pltpu.make_async_copy(a, b, local_sem.at[k]) for k, (a, b) in enumerate(pairs)]
    for load in loads:
        load.start()

    leads = jnp.where(lane == GROUP - 1, NZ - GROUP * (group + 1), 0)
    loads[0].wait()
    mine = x * NC + c
    gathered[mine] = diag[...]
    pl.semaphore_wait(barrier, 14 + jnp.where(s > 0, 1, 0) + (GROUP - 1 - lane) + leads)

    for device in xc_peers:
        pltpu.make_async_remote_copy(
            src_ref=diag, dst_ref=gathered.at[mine], send_sem=xc_sem.at[0], recv_sem=xc_sem.at[1],
            device_id=device, device_id_type=MESH,
        ).start()

    to_upper = [
        pltpu.make_async_remote_copy(
            src_ref=less_hbm.at[:, k, pl.ds(SURF, SURF), :], dst_ref=low_block.at[:, k],
            send_sem=halo_send.at[0, k], recv_sem=halo_recv.at[0, k], device_id=(e, s + 1), device_id_type=MESH,
        )
        for k in range(2)
    ]
    to_lower = [
        pltpu.make_async_remote_copy(
            src_ref=less_hbm.at[:, k, pl.ds(0, SURF), :], dst_ref=up_block.at[:, k],
            send_sem=halo_send.at[1, k], recv_sem=halo_recv.at[1, k], device_id=(e, s - 1), device_id_type=MESH,
        )
        for k in range(2)
    ]
    for k in range(2):

        @pl.when(s < NZ - 1)
        def _(k=k):
            to_upper[k].start()

        @pl.when(s > 0)
        def _(k=k):
            to_lower[k].start()

    @pl.when(s == 0)
    def _():
        low_block[...] = jnp.zeros_like(low_block)

    @pl.when(s == NZ - 1)
    def _():
        up_block[...] = jnp.zeros_like(up_block)

    for load in loads[1:5]:
        load.wait()
    rows = lax.broadcasted_iota(jnp.int32, (16, 16), 0)
    cols = lax.broadcasted_iota(jnp.int32, (16, 16), 1)
    energy_to = x * 32 + (rows // 2) * 4 + c * 2 + lax.rem(rows, 2)
    energy_from = (cols // 4) * 32 + y * 4 + lax.rem(cols, 4)
    gap = energy_from - energy_to
    coupling = jnp.zeros((16, 16), F32)
    for q in range(MODES):
        emitted = (gap == offset[q]).astype(F32)
        absorbed = (gap == -offset[q]).astype(F32)
        coupling = coupling + strength[q] * ((bose[q] + 1.0) * emitted + bose[q] * absorbed)

    loads[5].wait()
    loads[6].wait()
    slots = lax.broadcasted_iota(jnp.int32, (SURF, ORB), 0)
    for t in range(2):
        couple = jnp.zeros((SURF, ORB), F32)
        for k in range(NB):
            couple = couple + jnp.where(near[0, t, k : k + 1, :] == slots, hop[0, t, k : k + 1, :], 0.0)
        cph[pl.ds(t * SURF, SURF)], cpl[pl.ds(t * SURF, SURF)] = split(couple)
    loads[7].wait()
    for k in range(2):
        for b in range(2):
            for part in range(2):
                high, low = split(green[part, k, pl.ds(b * SURF, SURF), :])
                gh[k, b, pl.ds(part * SURF, SURF), :] = high
                gl[k, b, pl.ds(part * SURF, SURF), :] = low

    def arrived(buffer, count, sem):
        pltpu.make_async_copy(buffer.at[pl.ds(0, count)], buffer.at[pl.ds(0, count)], sem).wait()

    arrived(gathered, 7, xc_sem.at[0])
    arrived(gathered, 7, xc_sem.at[1])
    for j in range(8):
        for part in range(2):
            stacked[pl.ds(2 * j, 2), pl.ds(part * ORB, ORB)] = gathered[j, part]
    product = jnp.dot(coupling, stacked[...], precision=lax.Precision.HIGHEST, preferred_element_type=F32)
    for j in range(NY):
        partial[j] = product[2 * j : 2 * j + 2, :]
    for there, device in y_peers:
        pltpu.make_async_remote_copy(
            src_ref=partial.at[there], dst_ref=reduced.at[y], send_sem=y_sem.at[0], recv_sem=y_sem.at[1],
            device_id=device, device_id_type=MESH,
        ).start()
    reduced[y] = partial[y]

    for k in range(2):
        for b in range(2):
            high, low = split(dot3(gh[k, b], gl[k, b], cph[...], cpl[...], True))
            ch[k, b], cl[k, b] = high, low

    def surfaces(k):
        @pl.when(s > 0)
        def _():
            to_upper[k].wait_recv()

        @pl.when(s < NZ - 1)
        def _():
            to_lower[k].wait_recv()

        for t, block in ((0, low_block), (1, up_block)):
            real_high, real_low = split(block[0, k])
            imag_high, imag_low = split(block[1, k])

            def matrix(real, imag):
                return jnp.concatenate(
                    [jnp.concatenate([real, imag], axis=1), jnp.concatenate([-imag, real], axis=1)], axis=0
                )

            right_high, right_low = matrix(real_high, imag_high), matrix(real_low, imag_low)
            for b in range(2):

                def side(ref):
                    lanes = pl.ds(t * SURF, SURF)
                    return jnp.concatenate([ref[k, b, pl.ds(0, SURF), lanes], ref[k, b, pl.ds(SURF, SURF), lanes]], axis=1)

                high, low = split(dot3(side(ch), side(cl), right_high, right_low, False))
                for part in range(2):
                    there = (b, pl.ds(part * SURF, SURF), pl.ds(t * SURF, SURF))
                    wh[there] = high[:, part * SURF : (part + 1) * SURF]
                    wl[there] = low[:, part * SURF : (part + 1) * SURF]
        for b in range(2):
            quad = dot3(wh[b], wl[b], ch[k, b], cl[k, b], True)
            here = pl.ds(b * SURF, SURF)
            out_ref[0, k, here, :] = quad[:SURF, :SURF] + quad[SURF:, SURF:]
            out_ref[1, k, here, :] = quad[SURF:, :SURF] - quad[:SURF, SURF:]

    surfaces(0)

    arrived(partial, 7, y_sem.at[0])
    arrived(reduced, 7, y_sem.at[1])
    own = reduced[0]
    for j in range(1, NY):
        own = own + reduced[j]
    wide = 2 * ORB
    rate = jnp.broadcast_to(damp[...], (2, ORB))
    zout[0, :, pl.ds(0, wide)] = own
    zout[0, :, pl.ds(wide, ORB)] = rate
    in_group = [
        pltpu.make_async_remote_copy(
            src_ref=zout.at[0], dst_ref=zgroup.at[lane], send_sem=zs_sem.at[k], recv_sem=zr_sem.at[lane],
            device_id=(e, group * GROUP + k), device_id_type=MESH,
        )
        for k in range(1, GROUP)
    ]
    for k in range(1, GROUP):

        @pl.when(k > lane)
        def _(k=k):
            in_group[k - 1].start()

    surfaces(1)

    def from_slot(buffer, sems, k):
        return pltpu.make_async_copy(buffer.at[k], buffer.at[k], sems.at[k])

    def twice(value):
        return jnp.concatenate([value, value], axis=1)

    def gather_step(k, state):
        carried, decay = state
        from_slot(zgroup, zr_sem, k).wait()
        row = zgroup[k]
        step = row[:, wide:]
        return carried * twice(step) + row[:, :wide], decay * step

    carried, decay = lax.fori_loop(0, lane, gather_step, (jnp.zeros((2, wide), F32), jnp.ones((2, ORB), F32)))
    totals = [
        pltpu.make_async_remote_copy(
            src_ref=zout.at[1], dst_ref=ztotal.at[group], send_sem=lead_sem.at[k], recv_sem=total_sem.at[group],
            device_id=(e, jnp.int32(k)), device_id_type=MESH,
        )
        for k in range(GROUP, NZ)
    ]

    @pl.when(lane == GROUP - 1)
    def _():
        zout[1, :, pl.ds(0, wide)] = carried * twice(rate) + own
        zout[1, :, pl.ds(wide, ORB)] = decay * rate

    for k in range(NZ - 1, GROUP - 1, -1):

        @pl.when((lane == GROUP - 1) & (k // GROUP > group))
        def _(k=k):
            totals[k - GROUP].start()

    def total_step(k, total):
        from_slot(ztotal, total_sem, k).wait()
        row = ztotal[k]
        return total * twice(row[:, wide:]) + row[:, :wide]

    below = lax.fori_loop(0, group, total_step, jnp.zeros((2, wide), F32))
    sigma = own + carried + twice(decay) * below
    for part in range(2):
        sigma_ref[part] = sigma[:, part * ORB : (part + 1) * ORB]

    for k in range(2):
        sigma_real, sigma_imag = sigma[k : k + 1, :ORB], sigma[k : k + 1, ORB:]
        for b in range(2):
            here = pl.ds(b * SURF, SURF)
            green_real, green_imag = green[0, k, here, :], green[1, k, here, :]
            real_high, real_low = split(green_real * sigma_real - green_imag * sigma_imag)
            imag_high, imag_low = split(green_real * sigma_imag + green_imag * sigma_real)
            quad = dot3(
                jnp.concatenate([real_high, imag_high], axis=0), jnp.concatenate([real_low, imag_low], axis=0),
                gh[k, b], gl[k, b], True,
            )
            out_ref[0, k, here, :] += quad[:SURF, :SURF] + quad[SURF:, SURF:]
            out_ref[1, k, here, :] += quad[SURF:, :SURF] - quad[:SURF, SURF:]

    for k in range(1, GROUP):

        @pl.when(k > lane)
        def _(k=k):
            in_group[k - 1].wait_send()

    for k in range(GROUP, NZ):

        @pl.when((lane == GROUP - 1) & (k // GROUP > group))
        def _(k=k):
            totals[k - GROUP].wait_send()

    for k in range(2):

        @pl.when(s < NZ - 1)
        def _(k=k):
            to_upper[k].wait_send()

        @pl.when(s > 0)
        def _(k=k):
            to_lower[k].wait_send()


def local(*args):
    vmem, smem, dma = pltpu.VMEM, pltpu.SMEM, pltpu.SemaphoreType.DMA
    return pl.pallas_call(
        kernel,
        out_shape=(
            jax.ShapeDtypeStruct((2, 2, 2 * SURF, SURF), F32),
            jax.ShapeDtypeStruct((2, 2, ORB), F32),
        ),
        in_specs=[pl.BlockSpec(memory_space=pltpu.HBM)] * 9,
        out_specs=(pl.BlockSpec(memory_space=vmem), pl.BlockSpec(memory_space=vmem)),
        scratch_shapes=[
            vmem((2, 2, 2 * SURF, ORB), F32),
            vmem((2, 2, 2 * SURF, ORB), BF16),
            vmem((2, 2, 2 * SURF, ORB), BF16),
            vmem((2, 2, 2 * SURF, 2 * SURF), BF16),
            vmem((2, 2, 2 * SURF, 2 * SURF), BF16),
            vmem((2 * SURF, ORB), BF16),
            vmem((2 * SURF, ORB), BF16),
            vmem((2, 2 * SURF, 2 * SURF), BF16),
            vmem((2, 2 * SURF, 2 * SURF), BF16),
            vmem((1, 2, NB, ORB), jnp.int32),
            vmem((1, 2, NB, ORB), F32),
            vmem((1, ORB), F32),
            vmem((2, 2, ORB), F32),
            smem((MODES,), jnp.int32),
            smem((MODES,), F32),
            smem((MODES,), F32),
            vmem((8, 2, 2, ORB), F32),
            vmem((16, 2 * ORB), F32),
            vmem((NY, 2, 2 * ORB), F32),
            vmem((NY, 2, 2 * ORB), F32),
            vmem((2, 2, 3 * ORB), F32),
            vmem((GROUP, 2, 3 * ORB), F32),
            vmem((NZ // GROUP, 2, 3 * ORB), F32),
            vmem((2, 2, SURF, SURF), F32),
            vmem((2, 2, SURF, SURF), F32),
            dma((8,)),
            dma((2,)),
            dma((2,)),
            dma((GROUP,)),
            dma((GROUP,)),
            dma((NZ,)),
            dma((NZ // GROUP,)),
            dma((2, 2)),
            dma((2, 2)),
        ],
        compiler_params=pltpu.CompilerParams(
            collective_id=0, has_side_effects=True, vmem_limit_bytes=48 * 1024 * 1024
        ),
        cost_estimate=pl.CostEstimate(flops=5_000_000_000, bytes_accessed=4_000_000, transcendentals=0),
    )(*(pltpu.with_memory_space_constraint(arg, pltpu.HBM) for arg in args))


def solution(mesh):
    placed = (
        P(None, "energy", "slab", None),
        P(None, "energy", "slab", None),
        P(None, "energy", "slab"),
        P("slab", None, None, None),
        P("slab", None, None, None),
        P("slab", None),
        P(),
        P(),
        P(),
    )
    return jax.shard_map(
        local,
        mesh=mesh,
        in_specs=placed,
        out_specs=(P(None, "energy", "slab", None), P(None, "energy", "slab")),
        check_vma=False,
    )
```

time: 105 us -> 35.6 us (0.34)
  the two profiles are of different devices: /device:TPU:1 before, /device:TPU:256 now
where the time goes in v1:
time: 35.6 us; the launch traced here: 35.5 us
  Pallas kernels  33.4 us (94%)
  local copies, waits for them, and re-layouts  1.39 us (4%)
  between operations  0.64 us (2%)
    pallas_call x1, Pallas kernels, local(): pl.pallas_call(kernel, out_shape=(jax.ShapeDtypeStruct((2, 2, 2 * SURF, S...  33.4 us
    unnamed x2, local copies, waits for them, and re-layouts  1.39 us

profile of v1, /device:TPU:256, one launch (start us, length us, event | category | flops | bytes accessed | tf_op | source)
XLA Modules:
  0.0 35.5 jit_solution(15294312547415727789)
XLA Ops:
  0.6 33.4 %shard_map.104 = (f32[2,2,256,128]{3,2,1,0:T(8,128)S(1)}, f32[2,2,512]{2,1,0:T(2,128)S(1)}) custom-call(f32[2,2,256,512]{3,2,1,0:T(8,128)} %green_hbm.1, f32[2,2,256,128]{3,2,1,0:T(8,128)} %less_hbm.1, f32[2,2,512]{2,1,0:T(2,128)} %diag_hbm.1, s32[1,2,8,512]{3,2,1,0:T(8,128)} %near_hbm.1, f32[1,2,8,512]{3,2,1,0:T(8,128)} %hop_hbm.1, f32[1,512]{1,0:T(1,128)} %damp_hbm.1, ...), custom_call_target="tpu_custom_call" | custom-call | flops 5000000000 | bytes 4000000 | tf_op jit(solution)/shard_map/pallas_call | solution.py:328
  34.1 0.8 %copy.13 = f32[2,2,256,128]{3,2,1,0:T(8,128)} copy(f32[2,2,256,128]{3,2,1,0:T(8,128)S(1)} %get-tuple-element.4) | data formatting | bytes 1048576
  34.9 0.6 %copy.14 = f32[2,2,512]{2,1,0:T(2,128)} copy(f32[2,2,512]{2,1,0:T(2,128)S(1)} %get-tuple-element.5) | data formatting | bytes 16384

commit v2 on v1

--- a/solution.py
+++ b/solution.py
@@ -9,7 +9,7 @@
 F32 = jnp.float32
 BF16 = jnp.bfloat16
 NX, NY, NC, NZ = 4, 8, 2, 16
-GROUP = 4
+REACH = 8
 ORB = 512
 SURF = 128
 NB = 8
@@ -35,12 +35,11 @@
     out_ref, sigma_ref,
     green, gh, gl, ch, cl, cph, cpl, wh, wl,
     near, hop, damp, diag, offset, strength, bose,
-    gathered, stacked, partial, reduced, zout, zgroup, ztotal, low_block, up_block,
-    local_sem, xc_sem, y_sem, zs_sem, zr_sem, lead_sem, total_sem, halo_send, halo_recv,
+    gathered, stacked, partial, reduced, zout, zin, before, low_block, up_block,
+    local_sem, xc_sem, y_sem, zs_sem, zr_sem, halo_send, halo_recv, down_sem, up_sem,
 ):
     e, s = lax.axis_index("energy"), lax.axis_index("slab")
     x, y, c = e // (NY * NC), lax.rem(e // NC, NY), lax.rem(e, NC)
-    lane, group = lax.rem(s, GROUP), s // GROUP
 
     def at(px, py, pc):
         return (px * NY + py) * NC + pc
@@ -65,17 +64,9 @@
     def _():
         tell((e, s + 1))
 
-    for k in range(GROUP - 1):
-
-        @pl.when(k < lane)
-        def _(k=k):
-            tell((e, group * GROUP + k))
-
-    for k in range(NZ // GROUP - 1):
-
-        @pl.when(k < group)
-        def _(k=k):
-            tell((e, jnp.int32(k * GROUP + GROUP - 1)))
+    @pl.when(s > 0)
+    def _():
+        tell((e, s - 1))
 
     pairs = [
         (diag_hbm, diag), (damp_hbm, damp), (offset_hbm, offset), (strength_hbm, strength), (bose_hbm, bose),
@@ -85,11 +76,10 @@
     for load in loads:
         load.start()
 
-    leads = jnp.where(lane == GROUP - 1, NZ - GROUP * (group + 1), 0)
     loads[0].wait()
     mine = x * NC + c
     gathered[mine] = diag[...]
-    pl.semaphore_wait(barrier, 14 + jnp.where(s > 0, 1, 0) + (GROUP - 1 - lane) + leads)
+    pl.semaphore_wait(barrier, 14 + jnp.where(s > 0, 1, 0) + jnp.where(s < NZ - 1, 1, 0))
 
     for device in xc_peers:
         pltpu.make_async_remote_copy(
@@ -121,6 +111,19 @@
         def _(k=k):
             to_lower[k].start()
 
+    def pass_on(sem, step, when, there):
+        @pl.when(when)
+        def _():
+            pl.semaphore_signal(sem.at[step], inc=1, device_id=(e, there), device_id_type=MESH)
+
+    def hear(sem, step, when):
+        @pl.when(when)
+        def _():
+            pl.semaphore_wait(sem.at[step], 1)
+
+    pass_on(down_sem, 0, (s >= 1) & (s <= NZ - 2), s - 1)
+    pass_on(up_sem, 0, (s >= 1) & (s <= NZ - 2), s + 1)
+
     @pl.when(s == 0)
     def _():
         low_block[...] = jnp.zeros_like(low_block)
@@ -158,6 +161,11 @@
                 gh[k, b, pl.ds(part * SURF, SURF), :] = high
                 gl[k, b, pl.ds(part * SURF, SURF), :] = low
 
+    hear(down_sem, 0, s <= NZ - 3)
+    hear(up_sem, 0, s >= 2)
+    pass_on(down_sem, 1, (s >= 2) & (s <= NZ - 2), s - 2)
+    pass_on(up_sem, 1, (s >= 2) & (s <= NZ - 3), s + 2)
+
     def arrived(buffer, count, sem):
         pltpu.make_async_copy(buffer.at[pl.ds(0, count)], buffer.at[pl.ds(0, count)], sem).wait()
 
@@ -217,7 +225,12 @@
             out_ref[0, k, here, :] = quad[:SURF, :SURF] + quad[SURF:, SURF:]
             out_ref[1, k, here, :] = quad[SURF:, :SURF] - quad[:SURF, SURF:]
 
+    hear(down_sem, 1, s <= NZ - 4)
+    hear(up_sem, 1, s >= 4)
+    pass_on(down_sem, 2, (s >= 4) & (s <= NZ - 2), s - 4)
+
     surfaces(0)
+    surfaces(1)
 
     arrived(partial, 7, y_sem.at[0])
     arrived(reduced, 7, y_sem.at[1])
@@ -228,61 +241,51 @@
     rate = jnp.broadcast_to(damp[...], (2, ORB))
     zout[0, :, pl.ds(0, wide)] = own
     zout[0, :, pl.ds(wide, ORB)] = rate
-    in_group = [
+    ahead = [
         pltpu.make_async_remote_copy(
-            src_ref=zout.at[0], dst_ref=zgroup.at[lane], send_sem=zs_sem.at[k], recv_sem=zr_sem.at[lane],
-            device_id=(e, group * GROUP + k), device_id_type=MESH,
+            src_ref=zout.at[0 if d < REACH else 1], dst_ref=zin.at[d - 1], send_sem=zs_sem.at[d - 1],
+            recv_sem=zr_sem.at[d - 1], device_id=(e, s + d), device_id_type=MESH,
         )
-        for k in range(1, GROUP)
+        for d in range(1, REACH + 1)
     ]
-    for k in range(1, GROUP):
-
-        @pl.when(k > lane)
-        def _(k=k):
-            in_group[k - 1].start()
-
-    surfaces(1)
-
-    def from_slot(buffer, sems, k):
-        return pltpu.make_async_copy(buffer.at[k], buffer.at[k], sems.at[k])
+
+    def each_ahead(distances, act):
+        for d in distances:
+
+            @pl.when(s + d < NZ)
+            def _(d=d):
+                act(ahead[d - 1])
+
+    each_ahead(range(1, 5), lambda copy: copy.start())
+    hear(down_sem, 2, s <= NZ - 6)
+    each_ahead(range(5, REACH), lambda copy: copy.start())
+
+    def from_slot(k):
+        return pltpu.make_async_copy(zin.at[k], zin.at[k], zr_sem.at[k])
 
     def twice(value):
         return jnp.concatenate([value, value], axis=1)
 
-    def gather_step(k, state):
-        carried, decay = state
-        from_slot(zgroup, zr_sem, k).wait()
-        row = zgroup[k]
-        step = row[:, wide:]
-        return carried * twice(step) + row[:, :wide], decay * step
-
-    carried, decay = lax.fori_loop(0, lane, gather_step, (jnp.zeros((2, wide), F32), jnp.ones((2, ORB), F32)))
-    totals = [
-        pltpu.make_async_remote_copy(
-            src_ref=zout.at[1], dst_ref=ztotal.at[group], send_sem=lead_sem.at[k], recv_sem=total_sem.at[group],
-            device_id=(e, jnp.int32(k)), device_id_type=MESH,
-        )
-        for k in range(GROUP, NZ)
-    ]
-
-    @pl.when(lane == GROUP - 1)
+    before[...] = jnp.zeros_like(before)
+
+    @pl.when(s >= REACH)
     def _():
-        zout[1, :, pl.ds(0, wide)] = carried * twice(rate) + own
-        zout[1, :, pl.ds(wide, ORB)] = decay * rate
-
-    for k in range(NZ - 1, GROUP - 1, -1):
-
-        @pl.when((lane == GROUP - 1) & (k // GROUP > group))
-        def _(k=k):
-            totals[k - GROUP].start()
-
-    def total_step(k, total):
-        from_slot(ztotal, total_sem, k).wait()
-        row = ztotal[k]
-        return total * twice(row[:, wide:]) + row[:, :wide]
-
-    below = lax.fori_loop(0, group, total_step, jnp.zeros((2, wide), F32))
-    sigma = own + carried + twice(decay) * below
+        from_slot(REACH - 1).wait()
+        before[...] = zin[REACH - 1, :, pl.ds(0, wide)]
+
+    near_count = jnp.minimum(s, REACH - 1)
+
+    def scan_step(k, carried):
+        slot = near_count - 1 - k
+        from_slot(slot).wait()
+        row = zin[slot]
+        return carried * twice(row[:, wide:]) + row[:, :wide]
+
+    carried = lax.fori_loop(0, near_count, scan_step, before[...])
+    zout[1, :, pl.ds(0, wide)] = carried * twice(rate) + own
+    zout[1, :, pl.ds(wide, ORB)] = rate
+    each_ahead((REACH,), lambda copy: copy.start())
+    sigma = own + carried
     for part in range(2):
         sigma_ref[part] = sigma[:, part * ORB : (part + 1) * ORB]
 
@@ -300,17 +303,7 @@
             out_ref[0, k, here, :] += quad[:SURF, :SURF] + quad[SURF:, SURF:]
             out_ref[1, k, here, :] += quad[SURF:, :SURF] - quad[:SURF, SURF:]
 
-    for k in range(1, GROUP):
-
-        @pl.when(k > lane)
-        def _(k=k):
-            in_group[k - 1].wait_send()
-
-    for k in range(GROUP, NZ):
-
-        @pl.when((lane == GROUP - 1) & (k // GROUP > group))
-        def _(k=k):
-            totals[k - GROUP].wait_send()
+    each_ahead(range(1, REACH + 1), lambda copy: copy.wait_send())
 
     for k in range(2):
 
@@ -323,14 +316,23 @@
             to_lower[k].wait_send()
 
 
+def store(out_ref, sigma_ref, out_hbm, sigma_hbm, sem):
+    copies = [
+        pltpu.make_async_copy(out_ref, out_hbm, sem.at[0]),
+        pltpu.make_async_copy(sigma_ref, sigma_hbm, sem.at[1]),
+    ]
+    for copy in copies:
+        copy.start()
+    for copy in copies:
+        copy.wait()
+
+
 def local(*args):
     vmem, smem, dma = pltpu.VMEM, pltpu.SMEM, pltpu.SemaphoreType.DMA
-    return pl.pallas_call(
+    shapes = (jax.ShapeDtypeStruct((2, 2, 2 * SURF, SURF), F32), jax.ShapeDtypeStruct((2, 2, ORB), F32))
+    results = pl.pallas_call(
         kernel,
-        out_shape=(
-            jax.ShapeDtypeStruct((2, 2, 2 * SURF, SURF), F32),
-            jax.ShapeDtypeStruct((2, 2, ORB), F32),
-        ),
+        out_shape=shapes,
         in_specs=[pl.BlockSpec(memory_space=pltpu.HBM)] * 9,
         out_specs=(pl.BlockSpec(memory_space=vmem), pl.BlockSpec(memory_space=vmem)),
         scratch_shapes=[
@@ -355,25 +357,32 @@
             vmem((NY, 2, 2 * ORB), F32),
             vmem((NY, 2, 2 * ORB), F32),
             vmem((2, 2, 3 * ORB), F32),
-            vmem((GROUP, 2, 3 * ORB), F32),
-            vmem((NZ // GROUP, 2, 3 * ORB), F32),
+            vmem((REACH, 2, 3 * ORB), F32),
+            vmem((2, 2 * ORB), F32),
             vmem((2, 2, SURF, SURF), F32),
             vmem((2, 2, SURF, SURF), F32),
             dma((8,)),
             dma((2,)),
             dma((2,)),
-            dma((GROUP,)),
-            dma((GROUP,)),
-            dma((NZ,)),
-            dma((NZ // GROUP,)),
+            dma((REACH,)),
+            dma((REACH,)),
             dma((2, 2)),
             dma((2, 2)),
+            pltpu.SemaphoreType.REGULAR((3,)),
+            pltpu.SemaphoreType.REGULAR((2,)),
         ],
         compiler_params=pltpu.CompilerParams(
             collective_id=0, has_side_effects=True, vmem_limit_bytes=48 * 1024 * 1024
         ),
         cost_estimate=pl.CostEstimate(flops=5_000_000_000, bytes_accessed=4_000_000, transcendentals=0),
     )(*(pltpu.with_memory_space_constraint(arg, pltpu.HBM) for arg in args))
+    return pl.pallas_call(
+        store,
+        out_shape=shapes,
+        in_specs=[pl.BlockSpec(memory_space=vmem)] * 2,
+        out_specs=[pl.BlockSpec(memory_space=pl.ANY)] * 2,
+        scratch_shapes=[dma((2,))],
+    )(*(pltpu.with_memory_space_constraint(result, vmem) for result in results))
 
 
 def solution(mesh):

time: 35.6 us -> 29 us (0.81)
  the two profiles are of different devices: /device:TPU:256 before, /device:TPU:68 now
where the time goes in v2:
time: 29 us; the launch traced here: 28.9 us
  Pallas kernels  28.2 us (97%)
  between operations  0.64 us (2%)
    pallas_call x1, Pallas kernels, local(): pl.pallas_call(kernel, out_shape=shapes, in_specs=[pl.BlockSpec(memory_sp...  27.4 us
    pallas_call x1, Pallas kernels, local(): pl.pallas_call(store, out_shape=shapes, in_specs=[pl.BlockSpec(memory_spa...  0.81 us

profile of v2, /device:TPU:68, one launch (start us, length us, event | category | flops | bytes accessed | tf_op | source)
XLA Modules:
  0.0 28.9 jit_solution(3986851024805834663)
XLA Ops:
  0.6 27.4 %shard_map.104 = (f32[2,2,256,128]{3,2,1,0:T(8,128)S(1)}, f32[2,2,512]{2,1,0:T(2,128)S(1)}) custom-call(f32[2,2,256,512]{3,2,1,0:T(8,128)} %green_hbm.1, f32[2,2,256,128]{3,2,1,0:T(8,128)} %less_hbm.1, f32[2,2,512]{2,1,0:T(2,128)} %diag_hbm.1, s32[1,2,8,512]{3,2,1,0:T(8,128)} %near_hbm.1, f32[1,2,8,512]{3,2,1,0:T(8,128)} %hop_hbm.1, f32[1,512]{1,0:T(1,128)} %damp_hbm.1, ...), custom_call_target="tpu_custom_call" | custom-call | flops 5000000000 | bytes 4000000 | tf_op jit(solution)/shard_map/pallas_call | solution.py:333
  28.0 0.8 %shard_map.105 = (f32[2,2,256,128]{3,2,1,0:T(8,128)}, f32[2,2,512]{2,1,0:T(2,128)}) custom-call(f32[2,2,256,128]{3,2,1,0:T(8,128)S(1)} %get-tuple-element.4.out_ref, f32[2,2,512]{2,1,0:T(2,128)S(1)} %get-tuple-element.5.sigma_ref), custom_call_target="tpu_custom_call" | custom-call | tf_op jit(solution)/shard_map/pallas_call | solution.py:379

commit v3 on v2

--- a/solution.py
+++ b/solution.py
@@ -10,6 +10,9 @@
 BF16 = jnp.bfloat16
 NX, NY, NC, NZ = 4, 8, 2, 16
 REACH = 8
+NEAR = 3
+LATE = NZ - 4
+HALF = 8
 ORB = 512
 SURF = 128
 NB = 8
@@ -35,8 +38,8 @@
     out_ref, sigma_ref,
     green, gh, gl, ch, cl, cph, cpl, wh, wl,
     near, hop, damp, diag, offset, strength, bose,
-    gathered, stacked, partial, reduced, zout, zin, before, low_block, up_block,
-    local_sem, xc_sem, y_sem, zs_sem, zr_sem, halo_send, halo_recv, down_sem, up_sem,
+    gathered, stacked, partial, reduced, zout, zin, damp_in, before, low_block, up_block,
+    local_sem, xc_sem, y_sem, zs_sem, zr_sem, ds_sem, dr_sem, halo_send, halo_recv, down_sem, up_sem, ring_sem,
 ):
     e, s = lax.axis_index("energy"), lax.axis_index("slab")
     x, y, c = e // (NY * NC), lax.rem(e // NC, NY), lax.rem(e, NC)
@@ -45,7 +48,7 @@
         return (px * NY + py) * NC + pc
 
     xc_peers = []
-    for d in range(1, NX * NC):
+    for d in (4, 5, 2, 3, 6, 7, 1):
         px, pc = lax.rem(x + d // NC, NX), lax.rem(c + d % NC, NC)
         xc_peers.append((at(px, y, pc), s))
     y_peers = [(lax.rem(y + d, NY), (at(x, lax.rem(y + d, NY), c), s)) for d in range(1, NY)]
@@ -54,32 +57,30 @@
 
     def tell(device):
         pl.semaphore_signal(barrier, inc=1, device_id=device, device_id_type=MESH)
-
-    for _, device in y_peers:
-        tell(device)
-    for device in xc_peers:
-        tell(device)
-
-    @pl.when(s < NZ - 1)
-    def _():
-        tell((e, s + 1))
-
-    @pl.when(s > 0)
-    def _():
-        tell((e, s - 1))
 
     pairs = [
         (diag_hbm, diag), (damp_hbm, damp), (offset_hbm, offset), (strength_hbm, strength), (bose_hbm, bose),
         (near_hbm, near), (hop_hbm, hop), (green_hbm, green),
     ]
     loads = [pltpu.make_async_copy(a, b, local_sem.at[k]) for k, (a, b) in enumerate(pairs)]
-    for load in loads:
-        load.start()
+    loads[0].start()
+    for device in xc_peers:
+        tell(device)
+    for d in (1, NY - 1):
+        tell(y_peers[d - 1][1])
+
+    @pl.when(s < NZ - 1)
+    def _():
+        tell((e, s + 1))
+
+    @pl.when(s > 0)
+    def _():
+        tell((e, s - 1))
 
     loads[0].wait()
     mine = x * NC + c
     gathered[mine] = diag[...]
-    pl.semaphore_wait(barrier, 14 + jnp.where(s > 0, 1, 0) + jnp.where(s < NZ - 1, 1, 0))
+    pl.semaphore_wait(barrier, 9 + jnp.where(s > 0, 1, 0) + jnp.where(s < NZ - 1, 1, 0))
 
     for device in xc_peers:
         pltpu.make_async_remote_copy(
@@ -111,6 +112,9 @@
         def _(k=k):
             to_lower[k].start()
 
+    for load in loads[1:]:
+        load.start()
+
     def pass_on(sem, step, when, there):
         @pl.when(when)
         def _():
@@ -121,6 +125,15 @@
         def _():
             pl.semaphore_wait(sem.at[step], 1)
 
+    def ring_round(step):
+        for way, d in ((0, step), (1, NY - step)):
+            pl.semaphore_signal(ring_sem.at[step - 1, way], inc=1, device_id=y_peers[d - 1][1], device_id_type=MESH)
+
+    def ring_wait(step):
+        for way in range(2):
+            pl.semaphore_wait(ring_sem.at[step - 1, way], 1)
+
+    ring_round(1)
     pass_on(down_sem, 0, (s >= 1) & (s <= NZ - 2), s - 1)
     pass_on(up_sem, 0, (s >= 1) & (s <= NZ - 2), s + 1)
 
@@ -161,15 +174,16 @@
                 gh[k, b, pl.ds(part * SURF, SURF), :] = high
                 gl[k, b, pl.ds(part * SURF, SURF), :] = low
 
+    ring_wait(1)
+    ring_round(2)
     hear(down_sem, 0, s <= NZ - 3)
     hear(up_sem, 0, s >= 2)
     pass_on(down_sem, 1, (s >= 2) & (s <= NZ - 2), s - 2)
-    pass_on(up_sem, 1, (s >= 2) & (s <= NZ - 3), s + 2)
+    pass_on(up_sem, 1, (s >= LATE - 3) & (s <= NZ - 4), s + 2)
 
     def arrived(buffer, count, sem):
         pltpu.make_async_copy(buffer.at[pl.ds(0, count)], buffer.at[pl.ds(0, count)], sem).wait()
 
-    arrived(gathered, 7, xc_sem.at[0])
     arrived(gathered, 7, xc_sem.at[1])
     for j in range(8):
         for part in range(2):
@@ -177,12 +191,41 @@
     product = jnp.dot(coupling, stacked[...], precision=lax.Precision.HIGHEST, preferred_element_type=F32)
     for j in range(NY):
         partial[j] = product[2 * j : 2 * j + 2, :]
-    for there, device in y_peers:
+    ring_wait(2)
+    for d in (4, 3, 5, 2, 6, 1, 7):
+        there, device = y_peers[d - 1]
         pltpu.make_async_remote_copy(
             src_ref=partial.at[there], dst_ref=reduced.at[y], send_sem=y_sem.at[0], recv_sem=y_sem.at[1],
             device_id=device, device_id_type=MESH,
         ).start()
     reduced[y] = partial[y]
+
+    hear(down_sem, 1, s <= NZ - 4)
+    hear(up_sem, 1, (s >= LATE - 1) & (s <= NZ - 2))
+    pass_on(down_sem, 2, (s >= LATE - 1) & (s <= NZ - 2), s - 4)
+    damps = [
+        pltpu.make_async_remote_copy(
+            src_ref=damp, dst_ref=damp_in.at[d - 1], send_sem=ds_sem.at[d - 1], recv_sem=dr_sem.at[d - 1],
+            device_id=(e, s + d), device_id_type=MESH,
+        )
+        for d in range(1, REACH)
+    ]
+
+    def each_ahead(copies, distances, act):
+        for d in distances:
+
+            @pl.when((s + d < NZ) & ((d <= NEAR) | (s >= HALF)))
+            def _(d=d):
+                act(copies[d - 1])
+
+    def each_carry(distances, act):
+        for d in distances:
+
+            @pl.when((s == HALF - 1) | ((d == 4) & (s < HALF)))
+            def _(d=d):
+                act(carries[d - 4])
+
+    each_ahead(damps, range(1, 5), lambda copy: copy.start())
 
     for k in range(2):
         for b in range(2):
@@ -225,66 +268,61 @@
             out_ref[0, k, here, :] = quad[:SURF, :SURF] + quad[SURF:, SURF:]
             out_ref[1, k, here, :] = quad[SURF:, :SURF] - quad[:SURF, SURF:]
 
-    hear(down_sem, 1, s <= NZ - 4)
-    hear(up_sem, 1, s >= 4)
-    pass_on(down_sem, 2, (s >= 4) & (s <= NZ - 2), s - 4)
-
-    surfaces(0)
-    surfaces(1)
-
-    arrived(partial, 7, y_sem.at[0])
+    @pl.when(s == 0)
+    def _():
+        surfaces(0)
+        surfaces(1)
+
     arrived(reduced, 7, y_sem.at[1])
     own = reduced[0]
     for j in range(1, NY):
         own = own + reduced[j]
-    wide = 2 * ORB
-    rate = jnp.broadcast_to(damp[...], (2, ORB))
-    zout[0, :, pl.ds(0, wide)] = own
-    zout[0, :, pl.ds(wide, ORB)] = rate
-    ahead = [
-        pltpu.make_async_remote_copy(
-            src_ref=zout.at[0 if d < REACH else 1], dst_ref=zin.at[d - 1], send_sem=zs_sem.at[d - 1],
-            recv_sem=zr_sem.at[d - 1], device_id=(e, s + d), device_id_type=MESH,
+    zout[0] = own
+
+    def to_higher(part, d):
+        return pltpu.make_async_remote_copy(
+            src_ref=zout.at[part], dst_ref=zin.at[d - 1], send_sem=zs_sem.at[d - 1], recv_sem=zr_sem.at[d - 1],
+            device_id=(e, s + d), device_id_type=MESH,
         )
-        for d in range(1, REACH + 1)
-    ]
-
-    def each_ahead(distances, act):
-        for d in distances:
-
-            @pl.when(s + d < NZ)
-            def _(d=d):
-                act(ahead[d - 1])
-
-    each_ahead(range(1, 5), lambda copy: copy.start())
-    hear(down_sem, 2, s <= NZ - 6)
-    each_ahead(range(5, REACH), lambda copy: copy.start())
-
-    def from_slot(k):
-        return pltpu.make_async_copy(zin.at[k], zin.at[k], zr_sem.at[k])
-
-    def twice(value):
-        return jnp.concatenate([value, value], axis=1)
+
+    ahead = [to_higher(0, d) for d in range(1, REACH)]
+    carries = [to_higher(1, d) for d in range(4, REACH + 1)]
+    each_ahead(ahead, range(1, 5), lambda copy: copy.start())
+    hear(down_sem, 2, (s >= HALF) & (s <= NZ - 6))
+    each_ahead(damps, range(5, REACH), lambda copy: copy.start())
+    each_ahead(ahead, range(5, REACH), lambda copy: copy.start())
+
+    @pl.when(s > 0)
+    def _():
+        surfaces(0)
+        surfaces(1)
+
+    def from_slot(buffer, sem, k):
+        return pltpu.make_async_copy(buffer.at[k], buffer.at[k], sem.at[k])
 
     before[...] = jnp.zeros_like(before)
 
-    @pl.when(s >= REACH)
-    def _():
-        from_slot(REACH - 1).wait()
-        before[...] = zin[REACH - 1, :, pl.ds(0, wide)]
-
-    near_count = jnp.minimum(s, REACH - 1)
+    count = jnp.where(s < LATE, jnp.minimum(s, NEAR), s - HALF)
+
+    @pl.when(s > NEAR)
+    def _():
+        from_slot(zin, zr_sem, count).wait()
+        before[...] = zin[count]
+
+    def decayed(value, rate):
+        return value * jnp.concatenate([rate, rate], axis=1)
 
     def scan_step(k, carried):
-        slot = near_count - 1 - k
-        from_slot(slot).wait()
-        row = zin[slot]
-        return carried * twice(row[:, wide:]) + row[:, :wide]
-
-    carried = lax.fori_loop(0, near_count, scan_step, before[...])
-    zout[1, :, pl.ds(0, wide)] = carried * twice(rate) + own
-    zout[1, :, pl.ds(wide, ORB)] = rate
-    each_ahead((REACH,), lambda copy: copy.start())
+        slot = count - 1 - k
+        from_slot(zin, zr_sem, slot).wait()
+        from_slot(damp_in, dr_sem, slot).wait()
+        return decayed(carried, damp_in[slot]) + zin[slot]
+
+    carried = lax.fori_loop(0, count, scan_step, before[...])
+    zout[1] = decayed(carried, damp[...]) + own
+    each_carry((4,), lambda copy: copy.start())
+    hear(down_sem, 2, s == HALF - 1)
+    each_carry(range(5, REACH + 1), lambda copy: copy.start())
     sigma = own + carried
     for part in range(2):
         sigma_ref[part] = sigma[:, part * ORB : (part + 1) * ORB]
@@ -303,7 +341,11 @@
             out_ref[0, k, here, :] += quad[:SURF, :SURF] + quad[SURF:, SURF:]
             out_ref[1, k, here, :] += quad[SURF:, :SURF] - quad[:SURF, SURF:]
 
-    each_ahead(range(1, REACH + 1), lambda copy: copy.wait_send())
+    arrived(gathered, 7, xc_sem.at[0])
+    arrived(partial, 7, y_sem.at[0])
+    each_ahead(damps, range(1, REACH), lambda copy: copy.wait_send())
+    each_ahead(ahead, range(1, REACH), lambda copy: copy.wait_send())
+    each_carry(range(4, REACH + 1), lambda copy: copy.wait_send())
 
     for k in range(2):
 
@@ -356,8 +398,9 @@
             vmem((16, 2 * ORB), F32),
             vmem((NY, 2, 2 * ORB), F32),
             vmem((NY, 2, 2 * ORB), F32),
-            vmem((2, 2, 3 * ORB), F32),
-            vmem((REACH, 2, 3 * ORB), F32),
+            vmem((2, 2, 2 * ORB), F32),
+            vmem((REACH, 2, 2 * ORB), F32),
+            vmem((REACH - 1, 1, ORB), F32),
             vmem((2, 2 * ORB), F32),
             vmem((2, 2, SURF, SURF), F32),
             vmem((2, 2, SURF, SURF), F32),
@@ -366,10 +409,13 @@
             dma((2,)),
             dma((REACH,)),
             dma((REACH,)),
+            dma((REACH - 1,)),
+            dma((REACH - 1,)),
             dma((2, 2)),
             dma((2, 2)),
             pltpu.SemaphoreType.REGULAR((3,)),
             pltpu.SemaphoreType.REGULAR((2,)),
+            pltpu.SemaphoreType.REGULAR((2, 2)),
         ],
         compiler_params=pltpu.CompilerParams(
             collective_id=0, has_side_effects=True, vmem_limit_bytes=48 * 1024 * 1024

time: 29 us -> 27.7 us (0.955)
  the two profiles are of different devices: /device:TPU:68 before, /device:TPU:64 now
where the time goes in v3:
time: 27.7 us; the launch traced here: 27.5 us
  Pallas kernels  26.9 us (97%)
  between operations  0.64 us (2%)
    pallas_call x1, Pallas kernels, local(): pl.pallas_call(kernel, out_shape=shapes, in_specs=[pl.BlockSpec(memory_sp...  26.1 us
    pallas_call x1, Pallas kernels, local(): pl.pallas_call(store, out_shape=shapes, in_specs=[pl.BlockSpec(memory_spa...  0.81 us

profile of v3, /device:TPU:64, one launch (start us, length us, event | category | flops | bytes accessed | tf_op | source)
XLA Modules:
  0.0 27.5 jit_solution(12746460728049911786)
XLA Ops:
  0.6 26.1 %shard_map.104 = (f32[2,2,256,128]{3,2,1,0:T(8,128)S(1)}, f32[2,2,512]{2,1,0:T(2,128)S(1)}) custom-call(f32[2,2,256,512]{3,2,1,0:T(8,128)} %green_hbm.1, f32[2,2,256,128]{3,2,1,0:T(8,128)} %less_hbm.1, f32[2,2,512]{2,1,0:T(2,128)} %diag_hbm.1, s32[1,2,8,512]{3,2,1,0:T(8,128)} %near_hbm.1, f32[1,2,8,512]{3,2,1,0:T(8,128)} %hop_hbm.1, f32[1,512]{1,0:T(1,128)} %damp_hbm.1, ...), custom_call_target="tpu_custom_call" | custom-call | flops 5000000000 | bytes 4000000 | tf_op jit(solution)/shard_map/pallas_call | solution.py:375
  26.7 0.8 %shard_map.105 = (f32[2,2,256,128]{3,2,1,0:T(8,128)}, f32[2,2,512]{2,1,0:T(2,128)}) custom-call(f32[2,2,256,128]{3,2,1,0:T(8,128)S(1)} %get-tuple-element.4.out_ref, f32[2,2,512]{2,1,0:T(2,128)S(1)} %get-tuple-element.5.sigma_ref), custom_call_target="tpu_custom_call" | custom-call | tf_op jit(solution)/shard_map/pallas_call | solution.py:425

commit v4 on v3

--- a/solution.py
+++ b/solution.py
@@ -30,7 +30,9 @@
     def one(left, right):
         return lax.dot_general(left, right, dims, preferred_element_type=F32)
 
-    return one(left_high, right_low) + one(left_low, right_high) + one(left_high, right_high)
+    rows = left_high.shape[0]
+    both = one(jnp.concatenate([left_low, left_high], axis=0), right_high)
+    return one(left_high, right_low) + both[:rows] + both[rows:]
 
 
 def kernel(
@@ -129,8 +131,8 @@
         for way, d in ((0, step), (1, NY - step)):
             pl.semaphore_signal(ring_sem.at[step - 1, way], inc=1, device_id=y_peers[d - 1][1], device_id_type=MESH)
 
-    def ring_wait(step):
-        for way in range(2):
+    def ring_wait(step, *ways):
+        for way in ways:
             pl.semaphore_wait(ring_sem.at[step - 1, way], 1)
 
     ring_round(1)
@@ -174,7 +176,7 @@
                 gh[k, b, pl.ds(part * SURF, SURF), :] = high
                 gl[k, b, pl.ds(part * SURF, SURF), :] = low
 
-    ring_wait(1)
+    ring_wait(1, 0, 1)
     ring_round(2)
     hear(down_sem, 0, s <= NZ - 3)
     hear(up_sem, 0, s >= 2)
@@ -191,8 +193,11 @@
     product = jnp.dot(coupling, stacked[...], precision=lax.Precision.HIGHEST, preferred_element_type=F32)
     for j in range(NY):
         partial[j] = product[2 * j : 2 * j + 2, :]
-    ring_wait(2)
-    for d in (4, 3, 5, 2, 6, 1, 7):
+    for d in (2, 6, 1, 7, 4, 5, 3):
+        if d == 4:
+            ring_wait(2, 0)
+        if d == 3:
+            ring_wait(2, 1)
         there, device = y_peers[d - 1]
         pltpu.make_async_remote_copy(
             src_ref=partial.at[there], dst_ref=reduced.at[y], send_sem=y_sem.at[0], recv_sem=y_sem.at[1],
@@ -268,7 +273,9 @@
             out_ref[0, k, here, :] = quad[:SURF, :SURF] + quad[SURF:, SURF:]
             out_ref[1, k, here, :] = quad[SURF:, :SURF] - quad[:SURF, SURF:]
 
-    @pl.when(s == 0)
+    early = (s == 0) & (e > 0)
+
+    @pl.when(early)
     def _():
         surfaces(0)
         surfaces(1)
@@ -292,7 +299,7 @@
     each_ahead(damps, range(5, REACH), lambda copy: copy.start())
     each_ahead(ahead, range(5, REACH), lambda copy: copy.start())
 
-    @pl.when(s > 0)
+    @pl.when(jnp.logical_not(early))
     def _():
         surfaces(0)
         surfaces(1)
@@ -359,10 +366,12 @@
 
 
 def store(out_ref, sigma_ref, out_hbm, sigma_hbm, sem):
-    copies = [
-        pltpu.make_async_copy(out_ref, out_hbm, sem.at[0]),
-        pltpu.make_async_copy(sigma_ref, sigma_hbm, sem.at[1]),
-    ]
+    copies = [pltpu.make_async_copy(sigma_ref, sigma_hbm, sem.at[0])]
+    for part in range(2):
+        for k in range(2):
+            for b in range(2):
+                here = (part, k, pl.ds(b * SURF, SURF))
+                copies.append(pltpu.make_async_copy(out_ref.at[here], out_hbm.at[here], sem.at[len(copies)]))
     for copy in copies:
         copy.start()
     for copy in copies:
@@ -427,7 +436,7 @@
         out_shape=shapes,
         in_specs=[pl.BlockSpec(memory_space=vmem)] * 2,
         out_specs=[pl.BlockSpec(memory_space=pl.ANY)] * 2,
-        scratch_shapes=[dma((2,))],
+        scratch_shapes=[dma((9,))],
     )(*(pltpu.with_memory_space_constraint(result, vmem) for result in results))
 
 

time: 27.7 us -> 27.6 us (level)
  no operation moved by 1% of the time
where the time goes in v4:
time: 27.6 us; the launch traced here: 27.3 us
  Pallas kernels  26.7 us (97%)
  between operations  0.64 us (2%)
    pallas_call x1, Pallas kernels, local(): pl.pallas_call(kernel, out_shape=shapes, in_specs=[pl.BlockSpec(memory_sp...  25.8 us
    pallas_call x1, Pallas kernels, local(): pl.pallas_call(store, out_shape=shapes, in_specs=[pl.BlockSpec(memory_spa...  0.86 us

profile of v4, /device:TPU:64, one launch (start us, length us, event | category | flops | bytes accessed | tf_op | source)
XLA Modules:
  0.0 27.3 jit_solution(8462835417218314037)
XLA Ops:
  0.6 25.8 %shard_map.104 = (f32[2,2,256,128]{3,2,1,0:T(8,128)S(1)}, f32[2,2,512]{2,1,0:T(2,128)S(1)}) custom-call(f32[2,2,256,512]{3,2,1,0:T(8,128)} %green_hbm.1, f32[2,2,256,128]{3,2,1,0:T(8,128)} %less_hbm.1, f32[2,2,512]{2,1,0:T(2,128)} %diag_hbm.1, s32[1,2,8,512]{3,2,1,0:T(8,128)} %near_hbm.1, f32[1,2,8,512]{3,2,1,0:T(8,128)} %hop_hbm.1, f32[1,512]{1,0:T(1,128)} %damp_hbm.1, ...), custom_call_target="tpu_custom_call" | custom-call | flops 5000000000 | bytes 4000000 | tf_op jit(solution)/shard_map/pallas_call | solution.py:384
  26.5 0.9 %shard_map.105 = (f32[2,2,256,128]{3,2,1,0:T(8,128)}, f32[2,2,512]{2,1,0:T(2,128)}) custom-call(f32[2,2,256,128]{3,2,1,0:T(8,128)S(1)} %get-tuple-element.4.out_ref, f32[2,2,512]{2,1,0:T(2,128)S(1)} %get-tuple-element.5.sigma_ref), custom_call_target="tpu_custom_call" | custom-call | tf_op jit(solution)/shard_map/pallas_call | solution.py:434

commit v5 on v4

--- a/solution.py
+++ b/solution.py
@@ -66,18 +66,19 @@
     ]
     loads = [pltpu.make_async_copy(a, b, local_sem.at[k]) for k, (a, b) in enumerate(pairs)]
     loads[0].start()
+    for d in (1, NY - 1):
+        tell(y_peers[d - 1][1])
+
+    @pl.when(s < NZ - 1)
+    def _():
+        tell((e, s + 1))
+
+    @pl.when(s > 0)
+    def _():
+        tell((e, s - 1))
+
     for device in xc_peers:
         tell(device)
-    for d in (1, NY - 1):
-        tell(y_peers[d - 1][1])
-
-    @pl.when(s < NZ - 1)
-    def _():
-        tell((e, s + 1))
-
-    @pl.when(s > 0)
-    def _():
-        tell((e, s - 1))
 
     loads[0].wait()
     mine = x * NC + c

time: 27.6 us -> 27.5 us (level)
  no operation moved by 1% of the time
where the time goes in v5:
time: 27.5 us; the launch traced here: 27.3 us
  Pallas kernels  26.7 us (97%)
  between operations  0.64 us (2%)
    pallas_call x1, Pallas kernels, local(): pl.pallas_call(kernel, out_shape=shapes, in_specs=[pl.BlockSpec(memory_sp...  25.8 us
    pallas_call x1, Pallas kernels, local(): pl.pallas_call(store, out_shape=shapes, in_specs=[pl.BlockSpec(memory_spa...  0.86 us

profile of v5, /device:TPU:64, one launch (start us, length us, event | category | flops | bytes accessed | tf_op | source)
XLA Modules:
  0.0 27.3 jit_solution(64318797677856913)
XLA Ops:
  0.6 25.8 %shard_map.104 = (f32[2,2,256,128]{3,2,1,0:T(8,128)S(1)}, f32[2,2,512]{2,1,0:T(2,128)S(1)}) custom-call(f32[2,2,256,512]{3,2,1,0:T(8,128)} %green_hbm.1, f32[2,2,256,128]{3,2,1,0:T(8,128)} %less_hbm.1, f32[2,2,512]{2,1,0:T(2,128)} %diag_hbm.1, s32[1,2,8,512]{3,2,1,0:T(8,128)} %near_hbm.1, f32[1,2,8,512]{3,2,1,0:T(8,128)} %hop_hbm.1, f32[1,512]{1,0:T(1,128)} %damp_hbm.1, ...), custom_call_target="tpu_custom_call" | custom-call | flops 5000000000 | bytes 4000000 | tf_op jit(solution)/shard_map/pallas_call | solution.py:385
  26.4 0.9 %shard_map.105 = (f32[2,2,256,128]{3,2,1,0:T(8,128)}, f32[2,2,512]{2,1,0:T(2,128)}) custom-call(f32[2,2,256,128]{3,2,1,0:T(8,128)S(1)} %get-tuple-element.4.out_ref, f32[2,2,512]{2,1,0:T(2,128)S(1)} %get-tuple-element.5.sigma_ref), custom_call_target="tpu_custom_call" | custom-call | tf_op jit(solution)/shard_map/pallas_call | solution.py:435
